TPU v7x, 128 devices: a whole 4x4x4 slice. The times are simulated.
128 devices in a mesh: ctx: 8 (over x, core), head: 16 (over z, y).
Axes of the slice: x: 4, y: 4, z: 4, core: 2. Of those that a mesh axis runs over, the one named last changes fastest.
Arguments:
- features: bfloat16 [2048, 6144], P('ctx', 'head'), may hold values from -6 to 6
- w_query: bfloat16 [6144, 8192], P(None, 'head'), may hold values from -0.078125 to 0.078125
- w_key: bfloat16 [6144, 8192], P(None, 'head'), may hold values from -0.078125 to 0.078125
- w_value: bfloat16 [6144, 8192], P(None, 'head'), may hold values from -0.078125 to 0.078125
- log_decay: float32 [64, 2048], P('head', 'ctx'), may hold values from -1 to 0, as said below
- d_out: bfloat16 [2048, 8192], P('ctx', 'head'), may hold values from -0.011962891 to 0.011962891
Outputs:
- d_features: bfloat16 [2048, 6144], P(('ctx', 'head'))
Inputs may be any that keep to these rules, and one draw needn't show every extreme that they name: `log_decay`: entries are negative or zero.
All inputs are finite; a program needn't handle non-finite values.
Results may differ from a plain program's by a relative error of at most 0.023.
Values may be sent and summed in bfloat16 or wider, within the bound.
No kernel may reach another device: no remote copies, remote signals or barrier semaphores. Data moves between devices by JAX's collectives and lax.ppermute only.
A program may use at most 128 MiB of HBM per device.

v0:
```python
import jax
import jax.numpy as jnp
from jax import lax
from jax.sharding import PartitionSpec as P

HI = lax.Precision.HIGHEST


def prefix(shard, axis, combine, identity, reverse):
    count, index = (lax.axis_size(axis), lax.axis_index(axis))
    everything = jax.tree.map(
        lambda part, kind: lax.all_gather(part.astype(kind), axis),
        shard,
        (jnp.bfloat16, jnp.bfloat16),
    )
    start = jax.tree.map(
        lambda part, zero: jnp.broadcast_to(jnp.asarray(zero, part.dtype), part.shape),
        shard,
        identity,
    )

    def lap(k, before):
        at = count - 1 - k if reverse else k
        reached = at > index if reverse else at < index
        new = combine(
            before, jax.tree.map(lambda part, own: part[at].astype(own.dtype), everything, shard)
        )
        return jax.tree.map(lambda a, b: jnp.where(reached, a, b), new, before)

    return lax.fori_loop(0, count, lap, start)


def split_heads(flat, head_count):
    return flat.reshape(flat.shape[0], head_count, -1).transpose(1, 0, 2)


def merge_heads(stacked):
    return stacked.transpose(1, 0, 2).reshape(stacked.shape[1], -1)


def forward_combine(earlier, later):
    return (earlier[0] + later[0], jnp.exp(later[0])[:, None, None] * earlier[1] + later[1])


def backward_combine(earlier, later):
    return (later[0] + earlier[0], later[1] + jnp.exp(later[0])[:, None, None] * earlier[1])


def shards(features, w_query, w_key, w_value, log_decay, d_out):
    f32 = jnp.float32
    row_count = features.shape[0]
    head_count = log_decay.shape[0]
    column_piece = lax.all_gather(features, "head", axis=1, tiled=True)
    query_sum = jnp.dot(column_piece, w_query, preferred_element_type=f32)
    key_sum = jnp.dot(column_piece, w_key, preferred_element_type=f32)
    value_sum = jnp.dot(column_piece, w_value, preferred_element_type=f32)
    queries = split_heads(query_sum.astype(jnp.bfloat16), head_count)
    keys_local = split_heads(key_sum.astype(jnp.bfloat16), head_count)
    values_local = split_heads(value_sum.astype(jnp.bfloat16), head_count)
    grads_out = split_heads(d_out, head_count)
    cumul = jnp.cumsum(log_decay, axis=1)
    total = cumul[:, -1]
    causal = jnp.tril(jnp.ones((row_count, row_count), dtype=bool))
    differ = cumul[:, :, None] - cumul[:, None, :]
    weights = jnp.where(causal[None], jnp.exp(jnp.minimum(differ, 0.0)), 0.0)
    tail = jnp.exp(total[:, None] - cumul)
    leading = jnp.exp(cumul)
    local_state = jnp.einsum(
        "hsi,hsj->hij",
        keys_local.astype(f32) * tail[:, :, None],
        values_local.astype(f32),
        precision=HI,
    )
    local_grad = jnp.einsum(
        "hti,htj->hij",
        queries.astype(f32) * leading[:, :, None],
        grads_out.astype(f32),
        precision=HI,
    )
    zero_total = jnp.zeros_like(total)
    zero_state = jnp.zeros_like(local_state)
    prefix_unused, state_in = prefix(
        (total, local_state), "ctx", forward_combine, (zero_total, zero_state), False
    )
    suffix_unused, grad_in = prefix(
        (total, local_grad), "ctx", backward_combine, (zero_total, zero_state), True
    )
    state_low = state_in.astype(jnp.bfloat16)
    grad_low = grad_in.astype(jnp.bfloat16)
    scores = (
        jnp.einsum("hti,hsi->hts", queries, keys_local, preferred_element_type=f32) * weights
    ).astype(jnp.bfloat16)
    mixing = (
        jnp.einsum("htj,hsj->hts", grads_out, values_local, preferred_element_type=f32) * weights
    ).astype(jnp.bfloat16)
    grad_query = jnp.einsum("hts,hsi->hti", mixing, keys_local, preferred_element_type=f32)
    grad_query = grad_query + leading[:, :, None] * jnp.einsum(
        "htj,hij->hti", grads_out, state_low, preferred_element_type=f32
    )
    grad_key = jnp.einsum("hts,hti->hsi", mixing, queries, preferred_element_type=f32)
    grad_key = grad_key + tail[:, :, None] * jnp.einsum(
        "hsj,hij->hsi", values_local, grad_low, preferred_element_type=f32
    )
    grad_value = jnp.einsum("hts,htj->hsj", scores, grads_out, preferred_element_type=f32)
    grad_value = grad_value + tail[:, :, None] * jnp.einsum(
        "hsi,hij->hsj", keys_local, grad_low, preferred_element_type=f32
    )
    query_grad_flat = merge_heads(grad_query.astype(jnp.bfloat16))
    key_grad_flat = merge_heads(grad_key.astype(jnp.bfloat16))
    value_grad_flat = merge_heads(grad_value.astype(jnp.bfloat16))
    summed = jnp.einsum("tc,dc->td", query_grad_flat, w_query, preferred_element_type=f32)
    summed = summed + jnp.einsum("tc,dc->td", key_grad_flat, w_key, preferred_element_type=f32)
    return lax.psum_scatter(
        (
            summed + jnp.einsum("tc,dc->td", value_grad_flat, w_value, preferred_element_type=f32)
        ).astype(jnp.bfloat16),
        "head",
        scatter_dimension=0,
        tiled=True,
    )


def solution(mesh):
    return jax.shard_map(
        shards,
        mesh=mesh,
        in_specs=(
            P("ctx", "head"),
            P(None, "head"),
            P(None, "head"),
            P(None, "head"),
            P("head", "ctx"),
            P("ctx", "head"),
        ),
        out_specs=P(("ctx", "head"), None),
        check_vma=False,
    )
```

profile of v0, /device:TPU:0, one launch (start us, length us, event | category | flops | bytes accessed | tf_op | source)
XLA Modules:
  0.0 224.2 jit_solution(17450735024143367338)
XLA Ops:
  8.0 1.2 reduce-window.6
  9.8 1.2 dynamic-slice
  12.0 14.7 %all-reduce = bf16[32]{0:T(256)(128)(2,1)S(1)} all-reduce(bf16[32]{0:T(256)(128)(2,1)S(1)} %dynamic-update-slice), channel_id=2, replica_groups=mesh['ctx'=8,'head'=16] {'ctx'}, use_global_device_ids=true, to_apply=%add | all-reduce | flops 32 | bytes 128
  26.8 1.1 copy.70
  28.0 36.8 %all-gather.7.cloned.1.call-done = bf16[256,6144]{1,0:T(8,128)(2,1)} async-done(((bf16[256,384]{1,0:T(8,128)(2,1)}), bf16[256,6144]{1,0:T(8,128)(2,1)}) %all-gather.7.cloned.1.call-update) | async-done | bytes 3145744 | tf_op jit(solution)/shard_map/all_gather | solution.py:53
  64.7 5.5 %fusion.17 = bf16[32,4,8,128]{3,2,1,0:T(8,128)(2,1)S(1)} fusion(bf16[256,6144]{1,0:T(8,128)(2,1)} %all-gather.7.cloned.1.call-done, bf16[6144,512]{1,0:T(8,128)(2,1)} %param.11), kind=kOutput, calls=%fused_computation.34 | convolution fusion | flops 1610743808 | bytes 9699328 | tf_op jit(solution)/shard_map/dot_general | solution.py:54
  70.2 1.4 convolution_convert_fusion.3
  71.8 5.7 %fusion.16 = bf16[32,4,8,128]{3,2,1,0:T(8,128)(2,1)S(1)} fusion(bf16[256,6144]{1,0:T(8,128)(2,1)} %all-gather.7.cloned.1.call-done, bf16[6144,512]{1,0:T(8,128)(2,1)} %param.12), kind=kOutput, calls=%fused_computation.33 | convolution fusion | flops 1610743808 | bytes 9699328 | tf_op jit(solution)/shard_map/dot_general | solution.py:55
  77.4 4.6 %fusion.15 = bf16[32,4,8,128]{3,2,1,0:T(8,128)(2,1)S(1)} fusion(bf16[256,6144]{1,0:T(8,128)(2,1)S(1)} %copy-done, bf16[6144,512]{1,0:T(8,128)(2,1)} %param.13), kind=kOutput, calls=%fused_computation.32 | convolution fusion | flops 1610743808 | bytes 9699328 | tf_op jit(solution)/shard_map/dot_general | solution.py:56
  82.1 1.5 convolution_convert_fusion.4
  85.3 9.1 %all-gather.11.cloned.1.call-done = bf16[32,128,128]{2,1,0:T(8,128)(2,1)} async-done(((bf16[4,128,128]{2,1,0:T(8,128)(2,1)}), bf16[32,128,128]{2,1,0:T(8,128)(2,1)}) %all-gather.11.cloned.1.call-update) | async-done | bytes 1048592 | tf_op jit(solution)/shard_map/all_gather | solution.py:12
  94.4 8.5 %while.31 = (s32[]{:T(128)}, f32[4,128,128]{2,1,0:T(8,128)S(1)}, s32[]{:T(128)}, bf16[8,4,128,128]{3,2,1,0:T(8,128)(2,1)}, bf16[8,4]{1,0:T(8,128)(2,1)S(1)}, /*index=5*/s32[]{:T(128)}, s32[]{:T(128)}, s32[]{:T(128)}, s32[]{:T(128)}) while((s32[]{:T(128)}, f32[4,128,128]{2,1,0:T(8,128)S(1)}, s32[]{:T(128)}, ...), condition=%wide.region_5.6_spmd.clone, body=%wide.region_4.5_spmd.clone.sunk | while | flops 327692 | bytes 655575 | solution.py:30
  95.5 1.0 fusion.67
  97.6 1.0 fusion.67
  98.7 1.0 fusion.67
  99.8 1.0 fusion.67
  100.8 1.0 fusion.67
  101.9 1.0 fusion.67
  102.9 16.5 %all-gather.9.cloned.1.call-done = bf16[32,128,128]{2,1,0:T(8,128)(2,1)} async-done(((bf16[4,128,128]{2,1,0:T(8,128)(2,1)}), bf16[32,128,128]{2,1,0:T(8,128)(2,1)}) %all-gather.9.cloned.1.call-update) | async-done | bytes 1048592 | tf_op jit(solution)/shard_map/all_gather | solution.py:12
  119.4 8.4 %while.30 = (s32[]{:T(128)}, f32[4,128,128]{2,1,0:T(8,128)S(1)}, s32[]{:T(128)}, bf16[8,4]{1,0:T(8,128)(2,1)S(1)}, bf16[8,4,128,128]{3,2,1,0:T(8,128)(2,1)}, /*index=5*/s32[]{:T(128)}, s32[]{:T(128)}) while((s32[]{:T(128)}, f32[4,128,128]{2,1,0:T(8,128)S(1)}, s32[]{:T(128)}, bf16[8,4]{1,0:T(8,128)(2,1)S(1)}, ...), condition=%wide.region_3.4_spmd.clone, body=%wide.region_2.3_spmd.clone.sunk | while | flops 327688 | bytes 655513 | solution.py:30
  128.6 4.8 %fusion.45 = f32[256,6144]{1,0:T(8,128)S(1)} fusion(bf16[256,512]{0,1:T(8,128)(2,1)S(1)} %bitcast.157, bf16[6144,512]{1,0:T(8,128)(2,1)} %param.11), kind=kOutput, calls=%fused_computation.72 | convolution fusion | flops 1610612736 | bytes 12845056 | tf_op jit(solution)/shard_map/tc,dc->td/dot_general | solution.py:111
  133.4 1.9 convolution_add_fusion.1
  135.3 6.3 %fusion.2 = bf16[256,6144]{1,0:T(8,128)(2,1)} fusion(f32[256,6144]{1,0:T(8,128)S(1)} %convolution_add_fusion.1, bf16[256,512]{0,1:T(8,128)(2,1)S(1)} %bitcast.155, bf16[6144,512]{1,0:T(8,128)(2,1)} %param.13), kind=kOutput, calls=%fused_computation.8 | convolution fusion | flops 1613758464 | bytes 15990784 | tf_op jit(solution)/shard_map/tc,dc->td/dot_general | solution.py:115
  141.6 76.0 %reduce-scatter.2.cloned.1.call-done = bf16[16,6144]{1,0:T(8,128)(2,1)} async-done(((bf16[256,6144]{1,0:T(8,128)(2,1)}), bf16[16,6144]{1,0:T(8,128)(2,1)}) %reduce-scatter.2.cloned.1.call-update) | async-done | bytes 196624 | tf_op jit(solution)/shard_map/reduce_scatter | solution.py:113
  (66 shorter events, 15.3 us)
Async XLA Ops:
  6.5 58.2 %all-gather.7.cloned.1.call-start = ((), (), s32[]{:S(2)}) async-start(), calls=%async_computation.1 | async-start | bytes 3342336 | tf_op jit(solution)/shard_map/all_gather | solution.py:53
  7.3 87.2 %all-gather.11.cloned.1.call-start = ((), (), s32[]{:S(2)}) async-start(), calls=%async_computation.4 | async-start | bytes 1179648 | tf_op jit(solution)/shard_map/all_gather | solution.py:12
  71.7 47.7 %all-gather.9.cloned.1.call-start = ((), (), s32[]{:S(2)}) async-start(), calls=%async_computation.3 | async-start | bytes 1179648 | tf_op jit(solution)/shard_map/all_gather | solution.py:12
  71.8 5.7 %copy-start = (bf16[256,6144]{1,0:T(8,128)(2,1)S(1)}, bf16[256,6144]{1,0:T(8,128)(2,1)}, u32[]{:S(2)}) copy-start(bf16[256,6144]{1,0:T(8,128)(2,1)} %all-gather.7.cloned.1.call-done) | copy-start | bytes 9437188
  85.1 132.6 %reduce-scatter.2.cloned.1.call-start = ((), (), s32[]{:S(2)}) async-start(), calls=%async_computation.2 | async-start | bytes 3342336 | tf_op jit(solution)/shard_map/reduce_scatter | solution.py:113
  128.3 5.1 %slice-start = ((s8[6291456]{0:T(1024)(128)(4,1)}), s8[4194304]{0:T(1024)(128)(4,1)S(1)}, s32[]{:S(2)}) async-start(s8[6291456]{0:T(1024)(128)(4,1)} %bitcast.153), calls=%async_computation.5 | async-start | bytes 8388608
  128.6 4.8 %slice-start.1 = ((s8[6291456]{0:T(1024)(128)(4,1)}), s8[2097152]{0:T(1024)(128)(4,1)S(1)}, s32[]{:S(2)}) async-start(s8[6291456]{0:T(1024)(128)(4,1)} %bitcast.153), calls=%async_computation.6 | async-start | bytes 4194304
Sparse Core Ops, SparseCore 0:
  9.5 55.1 all-gather.6
  71.8 22.5 all-gather.10
  96.1 23.1 all-gather.8
  141.8 75.8 reduce-scatter.1
where the time goes:
time: 225 us; the launch traced here: 224 us
  waiting for transfers between devices  139 us (62%)
  matrix products  33.9 us (15%)
  other arithmetic  17.8 us (8%)
  blocking collectives  14.7 us (7%)
  between operations  14 us (6%)
  local copies, waits for them, and re-layouts  3.84 us (2%)
    reduce_scatter x1, waiting for transfers between devices, shards(): lax.psum_scatter((summed + jnp.einsum('tc,dc->td', value_grad_flat, w_val...  76 us
    all_gather x1, waiting for transfers between devices, shards(): column_piece = lax.all_gather(features, 'head', axis=1, tiled=True)  36.8 us
    all_gather x2, waiting for transfers between devices, prefix(): lax.all_gather(part.astype(kind), axis)  25.6 us
    select_n x16, other arithmetic, lap(): return jax.tree.map(lambda a, b: jnp.where(reached, a, b), new, before)  16.2 us
    unnamed x1, blocking collectives  14.7 us
    dot_general x1, matrix products, shards(): jnp.einsum('tc,dc->td', value_grad_flat, w_value, preferred_element_type=...  6.29 us
    dot_general x1, matrix products, shards(): key_sum = jnp.dot(column_piece, w_key, preferred_element_type=f32)  5.67 us
    dot_general x1, matrix products, shards(): query_sum = jnp.dot(column_piece, w_query, preferred_element_type=f32)  5.52 us
  transfers between devices with their start and end apart: 4, of which 4 were waited for; matrix products, arithmetic and copies ran while one was open for 12% of the time, Pallas kernels for 0%

commit v1 on v0

--- a/solution.py
+++ b/solution.py
@@ -50,7 +50,12 @@
     f32 = jnp.float32
     row_count = features.shape[0]
     head_count = log_decay.shape[0]
-    column_piece = lax.all_gather(features, "head", axis=1, tiled=True)
+    bank = []
+    for _ in range(lax.axis_size("head")):
+        bank.append(features)
+    b_next = jnp.stack(bank, 0)
+    z_new = lax.all_to_all(b_next, "head", split_axis=0, concat_axis=0)
+    column_piece = jnp.concatenate(z_new, 1)
     query_sum = jnp.dot(column_piece, w_query, preferred_element_type=f32)
     key_sum = jnp.dot(column_piece, w_key, preferred_element_type=f32)
     value_sum = jnp.dot(column_piece, w_value, preferred_element_type=f32)

time: 225 us -> 233 us (1.036)
  waiting for transfers between devices: 139 us -> 129 us
  starting transfers between devices: 0.3 us -> 8.44 us
  matrix products: 33.9 us -> 39.8 us
  local copies, waits for them, and re-layouts: 3.84 us -> 7.69 us
    all_gather x1 -> x0, waiting for transfers between devices: 36.8 us -> none  [shards(): column_piece = lax.all_gather(features, 'head', axis=1, tiled=True)]
    all_to_all x0 -> x1, waiting for transfers between devices: none -> 27.2 us  [shards(): z_new = lax.all_to_all(b_next, 'head', split_axis=0, concat_axis=0)]
    all_to_all x0 -> x1, starting transfers between devices: none -> 8.13 us  [shards(): z_new = lax.all_to_all(b_next, 'head', split_axis=0, concat_axis=0)]
    dot_general x1, matrix products: 1.92 us -> 4.58 us  [shards(): jnp.einsum('tc,dc->td', key_grad_flat, w_key, preferred_element_type=f32)]
  transfers between devices with their start and end apart: 4 -> 4, of which waited for: 4 -> 4; matrix products, arithmetic and copies ran while one was open for 12% -> 11% of each run, Pallas kernels for 0% -> 0%
where the time goes in v1:
time: 233 us; the launch traced here: 232 us
  waiting for transfers between devices  129 us (55%)
  matrix products  39.8 us (17%)
  other arithmetic  17.8 us (8%)
  blocking collectives  14.9 us (6%)
  between operations  14.1 us (6%)
  starting transfers between devices  8.44 us (4%)
  local copies, waits for them, and re-layouts  7.69 us (3%)
    reduce_scatter x1, waiting for transfers between devices, shards(): lax.psum_scatter((summed + jnp.einsum('tc,dc->td', value_grad_flat, w_val...  76 us
    all_to_all x1, waiting for transfers between devices, shards(): z_new = lax.all_to_all(b_next, 'head', split_axis=0, concat_axis=0)  27.2 us
    all_gather x2, waiting for transfers between devices, prefix(): lax.all_gather(part.astype(kind), axis)  25.8 us
    select_n x16, other arithmetic, lap(): return jax.tree.map(lambda a, b: jnp.where(reached, a, b), new, before)  16.2 us
    unnamed x1, blocking collectives  14.9 us
    all_to_all x1, starting transfers between devices, shards(): z_new = lax.all_to_all(b_next, 'head', split_axis=0, concat_axis=0)  8.13 us
    dot_general x1, matrix products, shards(): jnp.einsum('tc,dc->td', value_grad_flat, w_value, preferred_element_type=...  6.5 us
    dot_general x1, matrix products, shards(): key_sum = jnp.dot(column_piece, w_key, preferred_element_type=f32)  5.28 us
  transfers between devices with their start and end apart: 4, of which 4 were waited for; matrix products, arithmetic and copies ran while one was open for 11% of the time, Pallas kernels for 0%

profile of v1, /device:TPU:0, one launch (start us, length us, event | category | flops | bytes accessed | tf_op | source)
XLA Modules:
  0.0 232.2 jit_solution(10773799359655721735)
XLA Ops:
  6.5 1.1 copy.40
  7.6 2.0 stack.2
  9.6 8.1 %all-to-all-start = ((bf16[16,256,384]{1,2,0:T(8,128)(2,1)}), bf16[16,256,384]{1,2,0:T(8,128)(2,1)S(1)}, u32[]{:S(2)}, u32[]{:S(2)}) async-start(bf16[16,256,384]{1,2,0:T(8,128)(2,1)} %stack.2), calls=%async_computation | async-start | bytes 6291456 | tf_op jit(solution)/shard_map/all_to_all | solution.py:57
  17.8 1.2 reduce-window.6
  21.1 14.9 %all-reduce = bf16[32]{0:T(256)(128)(2,1)S(1)} all-reduce(bf16[32]{0:T(256)(128)(2,1)S(1)} %dynamic-update-slice), channel_id=2, replica_groups=mesh['ctx'=8,'head'=16] {'ctx'}, use_global_device_ids=true, to_apply=%add | all-reduce | flops 32 | bytes 128
  36.1 1.8 copy.72
  38.0 27.2 %all-to-all-done = bf16[16,256,384]{1,2,0:T(8,128)(2,1)S(1)} async-done(((bf16[16,256,384]{1,2,0:T(8,128)(2,1)}), bf16[16,256,384]{1,2,0:T(8,128)(2,1)S(1)}, u32[]{:S(2)}, u32[]{:S(2)}) %all-to-all-start) | async-done | bytes 3145760 | tf_op jit(solution)/shard_map/all_to_all | solution.py:57
  65.2 5.3 %fusion.16 = bf16[32,4,8,128]{3,2,1,0:T(8,128)(2,1)} fusion(bf16[256,6144]{0,1:T(8,128)(2,1)S(1)} %bitcast.156, bf16[6144,512]{1,0:T(8,128)(2,1)} %param.12), kind=kOutput, calls=%fused_computation.33 | convolution fusion | flops 1610743808 | bytes 9699328 | tf_op jit(solution)/shard_map/dot_general | solution.py:60
  70.5 4.6 %fusion.17 = bf16[32,4,8,128]{3,2,1,0:T(8,128)(2,1)S(1)} fusion(bf16[256,6144]{0,1:T(8,128)(2,1)S(1)} %bitcast.157, bf16[6144,512]{1,0:T(8,128)(2,1)} %param.11), kind=kOutput, calls=%fused_computation.34 | convolution fusion | flops 1610743808 | bytes 9699328 | tf_op jit(solution)/shard_map/dot_general | solution.py:59
  75.9 1.5 convolution_convert_fusion.3
  77.4 4.6 %fusion.15 = bf16[32,4,8,128]{3,2,1,0:T(8,128)(2,1)S(1)} fusion(bf16[256,6144]{0,1:T(8,128)(2,1)S(1)} %bitcast.158, bf16[6144,512]{1,0:T(8,128)(2,1)} %param.13), kind=kOutput, calls=%fused_computation.32 | convolution fusion | flops 1610743808 | bytes 9699328 | tf_op jit(solution)/shard_map/dot_general | solution.py:61
  82.7 1.4 convolution_convert_fusion.4
  84.2 1.4 fusion.5
  85.6 1.3 convolution_bitcast_fusion.6
  87.0 1.3 convolution_bitcast_fusion.4
  88.3 1.7 convolution_bitcast_fusion.2
  90.3 9.3 %all-gather.8.cloned.1.call-done = bf16[32,128,128]{2,1,0:T(8,128)(2,1)} async-done(((bf16[4,128,128]{2,1,0:T(8,128)(2,1)}), bf16[32,128,128]{2,1,0:T(8,128)(2,1)}) %all-gather.8.cloned.1.call-update) | async-done | bytes 1048592 | tf_op jit(solution)/shard_map/all_gather | solution.py:12
  99.5 8.5 %while.31 = (s32[]{:T(128)}, f32[4,128,128]{2,1,0:T(8,128)S(1)}, s32[]{:T(128)}, bf16[8,4,128,128]{3,2,1,0:T(8,128)(2,1)}, bf16[8,4]{1,0:T(8,128)(2,1)S(1)}, /*index=5*/s32[]{:T(128)}, s32[]{:T(128)}, s32[]{:T(128)}, s32[]{:T(128)}) while((s32[]{:T(128)}, f32[4,128,128]{2,1,0:T(8,128)S(1)}, s32[]{:T(128)}, ...), condition=%wide.region_5.6_spmd.clone, body=%wide.region_4.5_spmd.clone.sunk | while | flops 327692 | bytes 655575 | solution.py:30
  108.0 16.5 %all-gather.6.cloned.1.call-done = bf16[32,128,128]{2,1,0:T(8,128)(2,1)} async-done(((bf16[4,128,128]{2,1,0:T(8,128)(2,1)}), bf16[32,128,128]{2,1,0:T(8,128)(2,1)}) %all-gather.6.cloned.1.call-update) | async-done | bytes 1048592 | tf_op jit(solution)/shard_map/all_gather | solution.py:12
  124.5 8.4 %while.30 = (s32[]{:T(128)}, f32[4,128,128]{2,1,0:T(8,128)S(1)}, s32[]{:T(128)}, bf16[8,4]{1,0:T(8,128)(2,1)S(1)}, bf16[8,4,128,128]{3,2,1,0:T(8,128)(2,1)}, /*index=5*/s32[]{:T(128)}, s32[]{:T(128)}) while((s32[]{:T(128)}, f32[4,128,128]{2,1,0:T(8,128)S(1)}, s32[]{:T(128)}, bf16[8,4]{1,0:T(8,128)(2,1)S(1)}, ...), condition=%wide.region_3.4_spmd.clone, body=%wide.region_2.3_spmd.clone.sunk | while | flops 327688 | bytes 655513 | solution.py:30
  133.7 4.8 %fusion.45 = f32[256,6144]{1,0:T(8,128)S(1)} fusion(bf16[256,512]{0,1:T(8,128)(2,1)S(1)} %bitcast.165, bf16[6144,512]{1,0:T(8,128)(2,1)} %param.11), kind=kOutput, calls=%fused_computation.72 | convolution fusion | flops 1610612736 | bytes 12845056 | tf_op jit(solution)/shard_map/tc,dc->td/dot_general | solution.py:116
  138.6 4.6 %convolution_add_fusion.1 = f32[256,6144]{1,0:T(8,128)} fusion(f32[256,6144]{1,0:T(8,128)S(1)} %fusion.45, bf16[256,512]{0,1:T(8,128)(2,1)S(1)} %bitcast.164, bf16[6144,512]{1,0:T(8,128)(2,1)S(1)} %bitcast.160), kind=kOutput, calls=%fused_computation.7 | convolution fusion | flops 1612185600 | bytes 19136512 | tf_op jit(solution)/shard_map/tc,dc->td/dot_general | solution.py:117
  143.2 6.5 %fusion.2 = bf16[256,6144]{1,0:T(8,128)(2,1)} fusion(f32[256,6144]{1,0:T(8,128)} %convolution_add_fusion.1, bf16[256,512]{0,1:T(8,128)(2,1)S(1)} %bitcast.163, bf16[6144,512]{1,0:T(8,128)(2,1)S(1)} %bitcast.162), kind=kOutput, calls=%fused_computation.8 | convolution fusion | flops 1613758464 | bytes 15990784 | tf_op jit(solution)/shard_map/tc,dc->td/dot_general | solution.py:120
  149.7 76.0 %reduce-scatter.2.cloned.1.call-done = bf16[16,6144]{1,0:T(8,128)(2,1)} async-done(((bf16[256,6144]{1,0:T(8,128)(2,1)}), bf16[16,6144]{1,0:T(8,128)(2,1)}) %reduce-scatter.2.cloned.1.call-update) | async-done | bytes 196624 | tf_op jit(solution)/shard_map/reduce_scatter | solution.py:118
  (90 shorter events, 20.5 us)
Async XLA Ops:
  6.5 13.1 %copy-start.9 = (u32[128]{0:T(128)S(1)}, u32[128]{0:T(128)}, u32[]{:S(2)}) copy-start(u32[128]{0:T(128)} %constant.85) | copy-start | bytes 1540
  6.5 11.3 %copy-start.8 = (f32[4,256]{1,0:T(4,128)S(1)}, f32[4,256]{1,0:T(4,128)}, u32[]{:S(2)}) copy-start(f32[4,256]{1,0:T(4,128)} %param.14) | copy-start | bytes 12292
  9.6 55.6 %all-to-all-start = ((bf16[16,256,384]{1,2,0:T(8,128)(2,1)}), bf16[16,256,384]{1,2,0:T(8,128)(2,1)S(1)}, u32[]{:S(2)}, u32[]{:S(2)}) async-start(bf16[16,256,384]{1,2,0:T(8,128)(2,1)} %stack.2), calls=%async_computation | async-start | bytes 6291456 | tf_op jit(solution)/shard_map/all_to_all | solution.py:57
  17.7 81.8 %all-gather.8.cloned.1.call-start = ((), (), s32[]{:S(2)}) async-start(), calls=%async_computation.4 | async-start | bytes 1179648 | tf_op jit(solution)/shard_map/all_gather | solution.py:12
  70.5 5.4 %copy-start.6 = (bf16[256,512]{0,1:T(8,128)(2,1)S(1)}, bf16[256,512]{0,1:T(8,128)(2,1)}, u32[]{:S(2)}) copy-start(bf16[256,512]{0,1:T(8,128)(2,1)} %copy.72) | copy-start | bytes 786436
  75.1 0.7 copy-start.5
  77.4 47.1 %all-gather.6.cloned.1.call-start = ((), (), s32[]{:S(2)}) async-start(), calls=%async_computation.3 | async-start | bytes 1179648 | tf_op jit(solution)/shard_map/all_gather | solution.py:12
  77.4 5.3 %copy-start.1 = (bf16[32,4,8,128]{3,2,1,0:T(8,128)(2,1)S(1)}, bf16[32,4,8,128]{3,2,1,0:T(8,128)(2,1)}, u32[]{:S(2)}) copy-start(bf16[32,4,8,128]{3,2,1,0:T(8,128)(2,1)} %fusion.16) | copy-start | bytes 786436
  82.0 0.7 copy-start.3
  82.1 42.4 %copy-start = (f32[4,128,128]{2,1,0:T(8,128)S(1)}, f32[4,128,128]{2,1,0:T(8,128)}, u32[]{:S(2)}) copy-start(f32[4,128,128]{2,1,0:T(8,128)} %custom-call) | copy-start | bytes 786436
  85.6 47.3 %copy-start.2 = (bf16[32,4,8,128]{3,2,1,0:T(8,128)(2,1)S(1)}, bf16[32,4,8,128]{3,2,1,0:T(8,128)(2,1)}, u32[]{:S(2)}) copy-start(bf16[32,4,8,128]{3,2,1,0:T(8,128)(2,1)} %fusion.16) | copy-start | bytes 786436
  86.9 46.3 %copy-start.4 = (bf16[32,4,8,128]{3,2,1,0:T(8,128)(2,1)S(1)}, bf16[32,4,8,128]{3,2,1,0:T(8,128)(2,1)}, u32[]{:S(2)}) copy-start(bf16[32,4,8,128]{3,2,1,0:T(8,128)(2,1)} %copy-done.3) | copy-start | bytes 786436
  88.3 45.2 %copy-start.7 = (bf16[256,512]{0,1:T(8,128)(2,1)S(1)}, bf16[256,512]{0,1:T(8,128)(2,1)}, u32[]{:S(2)}) copy-start(bf16[256,512]{0,1:T(8,128)(2,1)} %copy.72) | copy-start | bytes 786436
  90.0 135.7 %reduce-scatter.2.cloned.1.call-start = ((), (), s32[]{:S(2)}) async-start(), calls=%async_computation.2 | async-start | bytes 3342336 | tf_op jit(solution)/shard_map/reduce_scatter | solution.py:118
  133.5 5.1 %slice-start = ((s8[6291456]{0:T(1024)(128)(4,1)}), s8[4194304]{0:T(1024)(128)(4,1)S(1)}, s32[]{:S(2)}) async-start(s8[6291456]{0:T(1024)(128)(4,1)} %bitcast.159), calls=%async_computation.5 | async-start | bytes 8388608
  133.7 4.8 %slice-start.1 = ((s8[6291456]{0:T(1024)(128)(4,1)}), s8[2097152]{0:T(1024)(128)(4,1)S(1)}, s32[]{:S(2)}) async-start(s8[6291456]{0:T(1024)(128)(4,1)} %bitcast.159), calls=%async_computation.6 | async-start | bytes 4194304
  133.7 9.4 %slice-start.2 = ((s8[6291456]{0:T(1024)(128)(4,1)}), s8[4194304]{0:T(1024)(128)(4,1)S(1)}, s32[]{:S(2)}) async-start(s8[6291456]{0:T(1024)(128)(4,1)} %bitcast.161), calls=%async_computation.7 | async-start | bytes 8388608
  138.6 4.6 %slice-start.3 = ((s8[6291456]{0:T(1024)(128)(4,1)}), s8[2097152]{0:T(1024)(128)(4,1)S(1)}, s32[]{:S(2)}) async-start(s8[6291456]{0:T(1024)(128)(4,1)} %bitcast.161), calls=%async_computation.8 | async-start | bytes 4194304
Sparse Core Ops, SparseCore 0:
  77.5 22.0 all-gather.7
  101.3 23.1 all-gather.5
  149.8 75.8 reduce-scatter.1
